TPU v7x, 512 devices: a whole 4x4x16 slice. The times are simulated.
512 devices in a mesh: alt: 8 (over x, y_hi), strip: 64 (over z, y_lo, core).
Axes of the slice: x: 4, y: 4 (y_hi: 2, y_lo: 2; y = y_hi * 2 + y_lo), z: 16, core: 2. Of those that a mesh axis runs over, the one named last changes fastest.
Arguments:
- screens: bfloat16 [16, 512, 512], P('alt', 'strip'), may hold values from -2.390625 to 2.390625
- row_offset: int32 [2, 16, 2], replicated, may hold values from 0 to 341, as said below
- col_offset: int32 [2, 16, 2], replicated, may hold values from 0 to 341, as said below
- layer_bin: int32 [16], replicated, may hold values from 0 to 15
- illumination: float32 [16, 12800], P(None, ('alt', 'strip')), may hold values from 0.3 to 1
- reconstructor: bfloat16 [2, 12800, 6000], P(None, ('alt', 'strip')), may hold values from -0.0390625 to 0.0390625
- sat_code: int32 [6000], replicated, may hold values from 1 to 16
Outputs:
- slopes: float32 [2, 2, 12800], P(None, None, ('alt', 'strip'))
- commands: float32 [2, 6000], replicated
Inputs may be any that keep to these rules, and one draw needn't show every extreme that they name: Every footprint lies inside the screen: row_offset[f, l, g] + (319) shrink_l <= 511. Every footprint lies inside the screen: col_offset[f, l, g] + (319) shrink_l <= 511.
All inputs are finite; a program needn't handle non-finite values.
Results may differ from a plain program's by a relative error of at most 0.0028.
Values sent between devices are 32-bit elements; how exact they have to be, the bound alone decides.
No kernel may reach another device: no remote copies, remote signals or barrier semaphores. Data moves between devices by JAX's collectives and lax.ppermute only.
A program may use at most 64 MiB of HBM per device.

v0:
```python
import math
import jax
import jax.numpy as jnp
from jax import lax
from jax.sharding import PartitionSpec as P

LENSLETS = 80
PIXELS = 4
GUIDE_STARS = 2
FRAMES = 2
ACTUATORS = 6000
PUPIL_PIX = 320
WINDOW = 384
SUBAPS_ALL = 12800
highest = lax.Precision.HIGHEST
loop_gain = 0.5
code_step = 0.125
bin_step = 0.03125


def bilinear(offsets):
    return jnp.maximum(0.0, 1.0 - jnp.abs(offsets))


def dft_tables():
    padded = 2 * PIXELS
    freq_index = jnp.arange(padded * padded, dtype=jnp.int32)
    freq_row = freq_index // padded
    freq_col = freq_index % padded
    pix_index = jnp.arange(PIXELS * PIXELS, dtype=jnp.int32)
    pix_row = pix_index // PIXELS
    pix_col = pix_index % PIXELS
    turn_count = (
        freq_row[:, None] * pix_row[None, :] + freq_col[:, None] * pix_col[None, :]
    ) % padded
    angles = turn_count.astype(jnp.float32) * (2.0 * math.pi / padded)
    coord_row = ((freq_row + PIXELS) % padded - PIXELS).astype(jnp.float32)
    coord_col = ((freq_col + PIXELS) % padded - PIXELS).astype(jnp.float32)
    return (jnp.cos(angles), jnp.sin(angles), coord_row, coord_col)


def centroids(pupil_phase, illumination, tables):
    cosine, sine_table, coord_row, coord_col = tables
    field_re = illumination * jnp.cos(pupil_phase)
    field_im = illumination * jnp.sin(pupil_phase)
    real_part = jnp.dot(cosine, field_re, precision=highest) + jnp.dot(
        sine_table, field_im, precision=highest
    )
    imag_part = jnp.dot(cosine, field_im, precision=highest) - jnp.dot(
        sine_table, field_re, precision=highest
    )
    intensity = real_part * real_part + imag_part * imag_part
    flux_sum = jnp.sum(intensity, axis=0)
    slope_row = jnp.sum(intensity * coord_row[:, None], axis=0) / flux_sum
    slope_col = jnp.sum(intensity * coord_col[:, None], axis=0) / flux_sum
    return jnp.stack([slope_row, slope_col])


def shards(screens, row_offset, col_offset, layer_bin, illumination, reconstructor, sat_code):
    layer_dev = screens.shape[0]
    rows_here = screens.shape[1]
    count_here = illumination.shape[1]
    group_pos = lax.axis_index("alt")
    strip_pos = lax.axis_index("strip")
    row_global = strip_pos * rows_here + jnp.arange(rows_here, dtype=jnp.int32)
    pupil_idx = jnp.arange(PUPIL_PIX, dtype=jnp.float32)
    window_idx = jnp.arange(WINDOW, dtype=jnp.float32)
    widened_layers = [
        jnp.pad(screens[layer_no], ((0, 0), (0, WINDOW))) for layer_no in range(layer_dev)
    ]
    frame_terms = []
    for frame_no in range(FRAMES):
        running = jnp.zeros((PIXELS, PIXELS, GUIDE_STARS, LENSLETS, LENSLETS), jnp.float32)
        for layer_no in range(layer_dev):
            layer_pos = group_pos * layer_dev + layer_no
            tops = lax.dynamic_index_in_dim(row_offset[frame_no], layer_pos, 0, keepdims=False)
            lefts = lax.dynamic_index_in_dim(col_offset[frame_no], layer_pos, 0, keepdims=False)
            bin_value = lax.dynamic_index_in_dim(layer_bin, layer_pos, 0, keepdims=False)
            shrink = 1.0 - bin_value.astype(jnp.float32) * bin_step
            col_weights = bilinear(window_idx[None, :] - pupil_idx[:, None] * shrink)
            widened = widened_layers[layer_no]

            def cut_columns(left_col):
                return lax.dynamic_slice_in_dim(widened, left_col, WINDOW, 1)

            strips = jax.vmap(cut_columns)(lefts).astype(jnp.float32)
            across = jnp.einsum("drc,jc->drj", strips, col_weights, precision=highest)
            offsets = (row_global[None, :] - tops[:, None]).astype(jnp.float32)
            row_weights = bilinear(offsets[:, None, :] - pupil_idx[None, :, None] * shrink)
            running = running + jnp.einsum(
                "dapr,drbq->pqdab",
                row_weights.reshape(GUIDE_STARS, LENSLETS, PIXELS, rows_here),
                across.reshape(GUIDE_STARS, rows_here, LENSLETS, PIXELS),
                precision=highest,
            )
        frame_terms.append(running.reshape(PIXELS * PIXELS, SUBAPS_ALL))
    phase_terms = jnp.concatenate(frame_terms, axis=0)
    owned = lax.psum_scatter(phase_terms, ("alt", "strip"), scatter_dimension=1, tiled=True)
    pupil_phase = owned.reshape(FRAMES, PIXELS * PIXELS, count_here)
    tables = dft_tables()
    slopes = jnp.stack(
        [centroids(pupil_phase[frame_no], illumination, tables) for frame_no in range(FRAMES)]
    )
    rounded = slopes.astype(jnp.bfloat16).reshape(FRAMES, 2 * count_here)
    partial_value = jnp.dot(
        rounded,
        reconstructor.reshape(2 * count_here, ACTUATORS),
        preferred_element_type=jnp.float32,
    )
    updates = lax.psum(partial_value, ("alt", "strip"))
    limits = sat_code.astype(jnp.float32) * code_step
    first_cmd = jnp.clip(loop_gain * updates[0], -limits, limits)
    second_cmd = jnp.clip(first_cmd + loop_gain * updates[1], -limits, limits)
    return (slopes, jnp.stack([first_cmd, second_cmd]))


def solution(mesh):
    placed = (
        P("alt", "strip", None),
        P(),
        P(),
        P(),
        P(None, ("alt", "strip")),
        P(None, ("alt", "strip"), None),
        P(),
    )
    return jax.shard_map(
        shards,
        mesh=mesh,
        in_specs=placed,
        out_specs=(P(None, None, ("alt", "strip")), P()),
        check_vma=False,
    )
```

profile of v0, /device:TPU:1, one launch (start us, length us, event | category | flops | bytes accessed | tf_op | source)
XLA Modules:
  0.0 635.3 jit_solution(2373824298019678638)
XLA Ops:
  7.2 1.4 fusion.161
  10.0 0.7 fusion.159
  10.8 0.7 fusion.160
  11.8 0.7 slice_bitcast_fusion
  12.6 2.7 while.4
  13.2 0.7 bitcast_dynamic-update-slice_fusion.8
  14.6 0.7 bitcast_dynamic-update-slice_fusion.8
  15.5 2.5 while.5
  19.2 1.2 fusion.21
  20.5 1.2 fusion.1
  22.1 1.7 reshape.445
  24.2 2.7 while.6
  24.8 0.7 bitcast_dynamic-update-slice_fusion.10
  26.2 0.7 bitcast_dynamic-update-slice_fusion.10
  27.6 2.6 while.7
  28.2 0.7 bitcast_dynamic-update-slice_fusion.11
  29.5 0.7 bitcast_dynamic-update-slice_fusion.11
  30.8 1.2 fusion.18
  32.0 1.2 fusion
  33.7 1.7 reshape.448
  35.4 2.5 pad_maximum_fusion
  38.0 477.4 %all-reduce.9.cloned.1.call-done = f32[32,12800]{1,0:T(8,128)} async-done(((f32[32,12800]{1,0:T(8,128)}), f32[32,12800]{1,0:T(8,128)}) %all-reduce.9.cloned.1.call-update) | async-done | bytes 1638416
  515.4 1.1 fusion.84
  516.5 1.1 fusion.82
  517.6 1.1 fusion.80
  518.7 1.1 fusion.78
  519.9 1.1 fusion.4
  521.0 1.1 fusion.7
  522.2 1.1 fusion.6
  523.3 1.3 multiply_reduce_fusion.1
  525.0 102.0 %psum.7 = f32[2,6000]{1,0:T(2,128)S(1)} all-reduce(f32[2,6000]{1,0:T(2,128)S(1)} %convolution_bitcast_fusion), channel_id=1, replica_groups=mesh['alt'=8,'strip'=64] {'alt','strip'}, use_global_device_ids=true, to_apply=%region_7.8 | all-reduce | flops 12000 | bytes 96000 | tf_op jit(solution)/shard_map/psum | solution.py:110
  627.8 0.7 pad_maximum_fusion.1
  (73 shorter events, 11.6 us)
Async XLA Ops:
  7.2 517.5 %copy-start = (bf16[2,25,6000]{2,0,1:T(2,128)(2,1)S(1)}, bf16[2,25,6000]{2,0,1:T(2,128)(2,1)}, u32[]{:S(2)}) copy-start(bf16[2,25,6000]{2,0,1:T(2,128)(2,1)} %param.12) | copy-start | bytes 1800004
  7.2 508.2 %all-reduce.9.cloned.1.call-start = ((), (), s32[]{:S(2)}) async-start(), calls=%async_computation | async-start | bytes 3276800
  33.6 1.7 copy-start.1
  37.9 477.5 %copy-start.3 = (f32[16,25]{1,0:T(8,128)S(1)}, f32[16,25]{1,0:T(8,128)}, u32[]{:S(2)}) copy-start(f32[16,25]{1,0:T(8,128)} %param.11) | copy-start | bytes 4804
  37.9 589.2 %copy-start.2 = (s32[6000]{0:T(1024)S(1)}, s32[6000]{0:T(1024)}, u32[]{:S(2)}) copy-start(s32[6000]{0:T(1024)} %param.13) | copy-start | bytes 72004
Sparse Core Ops, SparseCore 0:
  38.0 477.3 all-reduce.8
where the time goes:
time: 636 us; the launch traced here: 635 us
  waiting for transfers between devices  477 us (75%)
  blocking collectives  102 us (16%)
  local copies, waits for them, and re-layouts  20.2 us (3%)
  matrix products  16.4 us (3%)
  between operations  15.7 us (2%)
    unnamed x2, waiting for transfers between devices  477 us
    psum x1, blocking collectives, shards(): updates = lax.psum(partial_value, ('alt', 'strip'))  102 us
  transfers between devices with their start and end apart: 1, of which 1 were waited for; matrix products, arithmetic and copies ran while one was open for 0% of the time, Pallas kernels for 0%

commit v1 on v0

--- a/solution.py
+++ b/solution.py
@@ -107,7 +107,7 @@
         reconstructor.reshape(2 * count_here, ACTUATORS),
         preferred_element_type=jnp.float32,
     )
-    updates = lax.psum(partial_value, ("alt", "strip"))
+    updates = lax.psum(lax.psum(partial_value, "strip"), "alt")
     limits = sat_code.astype(jnp.float32) * code_step
     first_cmd = jnp.clip(loop_gain * updates[0], -limits, limits)
     second_cmd = jnp.clip(first_cmd + loop_gain * updates[1], -limits, limits)

time: 636 us -> 781 us (1.23); the launches traced: 635 us -> 772 us
  blocking collectives: 102 us -> 238 us
    psum x1 -> x2, blocking collectives: 102 us -> 238 us  [shards(): updates = lax.psum(lax.psum(partial_value, 'strip'), 'alt')]
where the time goes in v1:
time: 781 us; the launch traced here: 772 us
  waiting for transfers between devices  477 us (61%)
  blocking collectives  238 us (30%)
  local copies, waits for them, and re-layouts  20.2 us (3%)
  matrix products  16.4 us (2%)
  between operations  15.7 us (2%)
    unnamed x2, waiting for transfers between devices  477 us
    psum x2, blocking collectives, shards(): updates = lax.psum(lax.psum(partial_value, 'strip'), 'alt')  238 us
  transfers between devices with their start and end apart: 1, of which 1 were waited for; matrix products, arithmetic and copies ran while one was open for 0% of the time, Pallas kernels for 0%

profile of v1, /device:TPU:1, one launch (start us, length us, event | category | flops | bytes accessed | tf_op | source)
XLA Modules:
  0.0 771.8 jit_solution(15213481787349528862)
XLA Ops:
  7.2 1.4 fusion.161
  10.0 0.7 fusion.159
  10.8 0.7 fusion.160
  11.8 0.7 slice_bitcast_fusion
  12.6 2.7 while.4
  13.2 0.7 bitcast_dynamic-update-slice_fusion.8
  14.6 0.7 bitcast_dynamic-update-slice_fusion.8
  15.5 2.5 while.5
  19.2 1.2 fusion.21
  20.5 1.2 fusion.1
  22.1 1.7 reshape.445
  24.2 2.7 while.6
  24.8 0.7 bitcast_dynamic-update-slice_fusion.10
  26.2 0.7 bitcast_dynamic-update-slice_fusion.10
  27.6 2.6 while.7
  28.2 0.7 bitcast_dynamic-update-slice_fusion.11
  29.5 0.7 bitcast_dynamic-update-slice_fusion.11
  30.8 1.2 fusion.18
  32.0 1.2 fusion
  33.7 1.7 reshape.448
  35.4 2.5 pad_maximum_fusion
  38.0 477.4 %all-reduce.9.cloned.1.call-done = f32[32,12800]{1,0:T(8,128)} async-done(((f32[32,12800]{1,0:T(8,128)}), f32[32,12800]{1,0:T(8,128)}) %all-reduce.9.cloned.1.call-update) | async-done | bytes 1638416
  515.4 1.1 fusion.84
  516.5 1.1 fusion.82
  517.6 1.1 fusion.80
  518.7 1.1 fusion.78
  519.9 1.1 fusion.4
  521.0 1.1 fusion.7
  522.2 1.1 fusion.6
  523.3 1.3 multiply_reduce_fusion.1
  525.0 205.0 %psum.14 = f32[2,6000]{1,0:T(2,128)S(1)} all-reduce(f32[2,6000]{1,0:T(2,128)S(1)} %convolution_bitcast_fusion), channel_id=1, replica_groups=mesh['alt'=8,'strip'=64] {'strip'}, use_global_device_ids=true, to_apply=%region_7.8 | all-reduce | flops 12000 | bytes 96000 | tf_op jit(solution)/shard_map/psum | solution.py:110
  730.0 33.5 %psum.15 = f32[2,6000]{1,0:T(2,128)S(1)} all-reduce(f32[2,6000]{1,0:T(2,128)S(1)} %psum.14), channel_id=1, replica_groups=mesh['alt'=8,'strip'=64] {'alt'}, use_global_device_ids=true, to_apply=%region_8.9 | all-reduce | flops 12000 | bytes 96000 | tf_op jit(solution)/shard_map/psum | solution.py:110
  (74 shorter events, 12.3 us)
Async XLA Ops:
  7.2 517.5 %copy-start = (bf16[2,25,6000]{2,0,1:T(2,128)(2,1)S(1)}, bf16[2,25,6000]{2,0,1:T(2,128)(2,1)}, u32[]{:S(2)}) copy-start(bf16[2,25,6000]{2,0,1:T(2,128)(2,1)} %param.12) | copy-start | bytes 1800004
  7.2 508.2 %all-reduce.9.cloned.1.call-start = ((), (), s32[]{:S(2)}) async-start(), calls=%async_computation | async-start | bytes 3276800
  33.6 1.7 copy-start.1
  37.9 477.5 %copy-start.3 = (f32[16,25]{1,0:T(8,128)S(1)}, f32[16,25]{1,0:T(8,128)}, u32[]{:S(2)}) copy-start(f32[16,25]{1,0:T(8,128)} %param.11) | copy-start | bytes 4804
  37.9 725.7 %copy-start.2 = (s32[6000]{0:T(1024)S(1)}, s32[6000]{0:T(1024)}, u32[]{:S(2)}) copy-start(s32[6000]{0:T(1024)} %param.13) | copy-start | bytes 72004
Sparse Core Ops, SparseCore 0:
  38.0 477.3 all-reduce.8
